TPU v7x, 32 devices: a whole 2x2x4 slice. The times are simulated.
32 devices in a mesh: ta: 4 (over y, core), gx: 8 (over z, x).
Axes of the slice: x: 2, y: 2, z: 4, core: 2. Of those that a mesh axis runs over, the one named last changes fastest.
Arguments:
- links: float32 [4, 2, 3, 3, 64, 16, 128], P(None, None, None, None, 'ta', 'gx'), may hold values from -1 to 1, as said below
Outputs:
- flowed: float32 [4, 2, 3, 3, 64, 16, 128], P(None, None, None, None, 'ta', 'gx')
- loop_table: float32 [5, 8], replicated
Inputs may be any that keep to these rules, and one draw needn't show every extreme that they name: `links`: every link is a special unitary 3 x 3 matrix, given by its real and imaginary parts.
All inputs are finite; a program needn't handle non-finite values.
Results may differ from a plain program's by a relative error of at most 0.0001.
Values sent between devices are 32-bit elements; how exact they have to be, the bound alone decides.
A program may use at most 192 MiB of HBM per device.

v0:
```python
import jax
import jax.numpy as jnp
from jax import lax
from jax.experimental import pallas as pl
from jax.experimental.pallas import tpu as pltpu
from jax.sharding import PartitionSpec as P

NY = 4
NZ = 32
LANES = NY * NZ
TMAX = 8
LEVELS = 5
EPS_FLOW = 0.05
TOP = 8


def product(a, b, da=False, db=False):
    out = []
    for i in range(3):
        row = []
        for j in range(3):
            rr = ii = ri = ir = None
            for k in range(3):
                ar, ai = a[k][i] if da else a[i][k]
                br, bi = b[j][k] if db else b[k][j]
                t = (ar * br, ai * bi, ar * bi, ai * br)
                if rr is None:
                    rr, ii, ri, ir = t
                else:
                    rr, ii, ri, ir = rr + t[0], ii + t[1], ri + t[2], ir + t[3]
            re = rr - ii if da == db else rr + ii
            if da and db:
                im = -(ri + ir)
            elif da:
                im = ri - ir
            elif db:
                im = ir - ri
            else:
                im = ri + ir
            row.append((re, im))
        out.append(row)
    return out


def cmul(a, b):
    return (a[0] * b[0] - a[1] * b[1], a[0] * b[1] + a[1] * b[0])


def third_row(first, second):
    out = []
    for j in range(3):
        k, l = (j + 1) % 3, (j + 2) % 3
        x, y = cmul(first[k], second[l]), cmul(first[l], second[k])
        out.append((x[0] - y[0], y[1] - x[1]))
    return out


def evolve(link, staple):
    m = product(link, staple)
    half = -0.5 * EPS_FLOW
    d = [-EPS_FLOW * m[i][i][1] for i in range(3)]
    trace = (d[0] + d[1] + d[2]) * (1.0 / 3.0)
    d = [v - trace for v in d]
    off = {}
    for i, j in ((0, 1), (0, 2), (1, 2)):
        off[i, j] = (half * (m[i][j][0] - m[j][i][0]), half * (m[i][j][1] + m[j][i][1]))
    a, b, c = off[0, 1], off[0, 2], off[1, 2]
    na, nb, nc = (v[0] * v[0] + v[1] * v[1] for v in (a, b, c))
    s = [-(d[0] * d[0] + na + nb), -(d[1] * d[1] + na + nc), -(d[2] * d[2] + nb + nc)]
    p = -0.5 * (s[0] + s[1] + s[2])

    def times_i(w, v):
        return (-w * v[1], w * v[0])

    conj = lambda v: (v[0], -v[1])
    add = lambda u, v: (u[0] + v[0], u[1] + v[1])
    sub = lambda u, v: (u[0] - v[0], u[1] - v[1])
    sq = {
        (0, 1): sub(times_i(d[0] + d[1], a), cmul(b, conj(c))),
        (0, 2): add(times_i(d[0] + d[2], b), cmul(a, c)),
        (1, 2): sub(times_i(d[1] + d[2], c), cmul(conj(a), b)),
    }
    cube = s[0] * d[0] + s[1] * d[1] + s[2] * d[2]
    for key in sq:
        u, v = sq[key], off[key]
        cube = cube - 2.0 * (u[1] * v[0] - u[0] * v[1])
    delta = cube * (1.0 / 3.0)
    e0 = (1.0 - delta * delta * (1.0 / 720.0), delta * (1.0 / 6.0 - p * (1.0 / 120.0)))
    e1 = (1.0 - p * (1.0 / 6.0 - p * (1.0 / 120.0)), delta * (1.0 / 24.0 - p * (1.0 / 360.0)))
    e2 = (0.5 - p * (1.0 / 24.0 - p * (1.0 / 720.0)), delta * (1.0 / 120.0))
    e = [[None] * 3 for _ in range(3)]
    for i in range(3):
        e[i][i] = (e0[0] - e1[1] * d[i] + e2[0] * s[i], e0[1] + e1[0] * d[i] + e2[1] * s[i])
    for i, j in off:
        e[i][j] = add(cmul(e1, off[i, j]), cmul(e2, sq[i, j]))
        x = off[i, j]
        e[j][i] = add(cmul(e1, (-x[0], x[1])), cmul(e2, conj(sq[i, j])))
    return product(e, link)


def roll(v, by, axis=1):
    by = by % v.shape[axis]
    return v if by == 0 else pltpu.roll(v, by, axis)


def shift_y(v, by):
    return roll(v, -NZ * by)


def shift_z(v, by, z):
    if by == 1:
        return jnp.where(z < NZ - 1, roll(v, -1), roll(v, NZ - 1))
    return jnp.where(z > 0, roll(v, 1), roll(v, 1 - NZ))


def flow_kernel(slices, split, links, left, right, before, after, corner_x, corner_t, out, packed, pad, sums, done, turn):
    halves = slices // 8
    end = TOP + slices

    def fill(c, _):
        for p in range(2):
            for h in range(halves):
                pad[c, 1 + p, TOP + 8 * h : TOP + 8 * h + 8, :] = links[c, pl.ds(16 * h + p, 8, stride=2), :]
            pad[c, 1 + p, TOP - 1 : TOP, :] = before[c, p : p + 1, :]
        return 0

    lax.fori_loop(0, 72, fill, 0)

    def fill_after(c, _):
        for p in range(2):
            pad[18 + c, 1 + p, end : end + 1, :] = after[c, p : p + 1, :]
        return 0

    lax.fori_loop(0, 54, fill_after, 0)

    def fill_corner(c, _):
        pad[18 + c, 0, end : end + 1, :] = corner_x[c, 0:1, :]
        pad[c, 3, TOP - 1 : TOP, :] = corner_t[c, 0:1, :]
        return 0

    lax.fori_loop(0, 18, fill_corner, 0)
    for source, plane, dirs in ((left, 0, (0, 1, 2, 3)), (right, 3, (0, 2, 3))):
        for n, d in enumerate(dirs):
            for h in range(halves):
                rows = [
                    [
                        tuple(source[12 * n + 6 * ri + 3 * i + j, 8 * h : 8 * h + 8, :] for ri in range(2))
                        for j in range(3)
                    ]
                    for i in range(2)
                ]
                rows.append(third_row(rows[0], rows[1]))
                for i in range(3):
                    for j in range(3):
                        for ri in range(2):
                            pad[18 * d + 9 * ri + 3 * i + j, plane, TOP + 8 * h : TOP + 8 * h + 8, :] = rows[i][j][ri]

    lane = lax.broadcasted_iota(jnp.int32, (8, LANES), 1)
    z = lane & (NZ - 1)

    def chunk(p, h):
        def load(d, *steps):
            dt = dx = 0
            rolls = []
            for axis, by in steps:
                if axis == 0:
                    dt += by
                elif axis == 1:
                    dx += by
                else:
                    rolls.append((axis, by))

            def one(c):
                v = pad[c, 1 + p + dx, TOP + 8 * h + dt : TOP + 8 * h + dt + 8, :]
                for axis, by in rolls:
                    v = shift_y(v, by) if axis == 2 else shift_z(v, by, z)
                return v

            return [[(one(18 * d + 3 * i + j), one(18 * d + 9 + 3 * i + j)) for j in range(3)] for i in range(3)]

        seen = set()

        def collect(d, value):
            for i in range(3):
                for j in range(3):
                    for ri in range(2):
                        at = 18 * d + 9 * ri + 3 * i + j
                        if at in seen:
                            sums[at] = sums[at] + value[i][j][ri]
                        else:
                            seen.add(at)
                            sums[at] = value[i][j][ri]

        def lower(m, v):
            if v < 2:
                q = product(load(m, (v, -1)), load(v, (m, 1), (v, -1)))
                collect(m, product(q, load(v, (v, -1)), da=True))
            else:
                q = product(product(load(m), load(v, (m, 1))), load(v), da=True)
                move = (lambda w: shift_y(w, -1)) if v == 2 else (lambda w: shift_z(w, -1, z))
                collect(m, [[(move(e[0]), move(e[1])) for e in row] for row in q])

        for m in range(4):
            for v in range(m + 1, 4):
                w = product(load(v, (m, 1)), load(m, (v, 1)), db=True)
                collect(m, product(w, load(v), db=True))
                collect(v, product(w, load(m), da=True, db=True))
                lower(m, v)
                lower(v, m)
        for m in range(4):
            staple = [
                [(sums[18 * m + 3 * i + j], sums[18 * m + 9 + 3 * i + j]) for j in range(3)] for i in range(3)
            ]
            new = evolve(load(m), staple)
            for i in range(3):
                for j in range(3):
                    for ri in range(2):
                        done[18 * m + 9 * ri + 3 * i + j, p, 8 * h : 8 * h + 8, :] = new[i][j][ri]

    def plane(p, _):
        for h in range(halves):
            chunk(p, h)
        return 0

    lax.fori_loop(0, 2, plane, 0)

    def back(c, _):
        for p in range(2):
            for h in range(halves):
                out[c, pl.ds(16 * h + p, 8, stride=2), :] = done[c, p, 8 * h : 8 * h + 8, :]
        return 0

    lax.fori_loop(0, 72, back, 0)

    width = LANES // split

    def pack(g, _):
        for p in range(2):
            for h in range(halves):
                held = [done[split * g + c, p, 8 * h : 8 * h + 8, :] for c in range(split)]
                for k in range(split):
                    mixed = None
                    for c in range(split):
                        moved = roll(held[c], width * (c - k))
                        mixed = moved if mixed is None else jnp.where(lane // width == c, moved, mixed)
                    turn[pl.ds(8 * 2 * split * h + 2 * k + p, 8, stride=2 * split), :] = mixed
        turned = jnp.transpose(turn[...])
        for c in range(split):
            packed[split * g + c] = turned[width * c : width * c + width, :]
        return 0

    lax.fori_loop(0, 36 // split, pack, 0)


def loop_kernel(blocks, per_slice, fields, out, early, lines, ahead, line_ahead):
    groups = fields.shape[2]
    lane_all = lax.broadcasted_iota(jnp.int32, (groups, LANES), 1)
    odd = (lane_all & 1) == 1
    lane = lax.broadcasted_iota(jnp.int32, (8, LANES), 1)
    slices = 16

    def forward_x(v, distance):
        if distance == 1:
            return jnp.where(odd, roll(roll(v, -1, 0), 1), roll(v, -1))
        return roll(v, -(distance // 2), 0)

    def forward_t(ref, lead, c, b, g, s):
        own = ref[lead, c, b, pl.ds(g, 8), :]
        if s == 0:
            return own
        following = ref[lead, c, lax.rem(b + 1, blocks), pl.ds(g, 8), :]
        slot = lane // per_slice if per_slice * slices == LANES else (lane // per_slice) % slices
        return roll(jnp.where(slot >= s, own, following), -per_slice * s)

    def first(b, _):
        for c in range(18):
            lines[0, c, b] = fields[18 + c, b]
            ahead[0, c, b] = forward_x(fields[c, b], 1)
        return 0

    lax.fori_loop(0, blocks, first, 0)
    for k in range(1, LEVELS):
        distance = 2 ** (k - 1)

        def grow(b, _):
            for c in range(18):
                ahead[k, c, b] = forward_x(ahead[k - 1, c, b], distance)
            own = [[(lines[k - 1, 3 * i + j, b], lines[k - 1, 9 + 3 * i + j, b]) for j in range(3)] for i in range(3)]
            far = [[tuple(forward_x(v, distance) for v in e) for e in row] for row in own]
            new = product(own, far)
            for i in range(3):
                for j in range(3):
                    for ri in range(2):
                        lines[k, 9 * ri + 3 * i + j, b] = new[i][j][ri]
            return 0

        lax.fori_loop(0, blocks, grow, 0)

    def advance(n, _):
        b = n // (groups // 8)
        g = pl.multiple_of((n % (groups // 8)) * 8, 8)
        for s in range(TMAX):
            for c in range(18):
                own = fields[c, b, pl.ds(g, 8), :]
                if s:
                    following = fields[c, lax.rem(b + 1, blocks), pl.ds(g, 8), :]
                    own = roll(jnp.where((lane // per_slice) % slices >= s, own, following), -per_slice * s)
                early[s, c, n] = own
        return 0

    cells = blocks * (groups // 8)
    lax.fori_loop(0, cells, advance, 0)

    def level(k, _):
        def cell(n, totals):
            b = n // (groups // 8)
            g = pl.multiple_of((n % (groups // 8)) * 8, 8)

            def matrix(get):
                return [[(get(3 * i + j), get(9 + 3 * i + j)) for j in range(3)] for i in range(3)]

            carried = matrix(lambda c: forward_t(lines, k, c, b, g, 0))
            new = []
            for extent in range(1, TMAX + 1):
                s = extent - 1
                carried = product(matrix(lambda c: early[s, c, n]), carried, da=True)
                carried = product(carried, matrix(lambda c: forward_t(ahead, k, c, b, g, s)))
                end = matrix(lambda c: forward_t(lines, k, c, b, g, extent))
                total = totals[s]
                for i in range(3):
                    for j in range(3):
                        total = total + (carried[i][j][0] * end[i][j][0] + carried[i][j][1] * end[i][j][1])
                new.append(total)
            return tuple(new)

        totals = lax.fori_loop(0, cells, cell, (jnp.zeros((8, LANES), jnp.float32),) * TMAX)
        for s in range(TMAX):
            out[k, pl.ds(s, 1), :] = jnp.sum(totals[s], axis=0, keepdims=True)
        return 0

    lax.fori_loop(0, LEVELS, level, 0)


def body(links):
    nta, ngx = lax.axis_size("ta"), lax.axis_size("gx")
    devices = nta * ngx
    slices = links.shape[4]
    vmem = pl.BlockSpec(memory_space=pltpu.VMEM)

    def send(value, dt, dx):
        perm = []
        for i in range(nta):
            for j in range(ngx):
                perm.append((i * ngx + j, ((i + dt) % nta) * ngx + (j + dx) % ngx))
        return lax.ppermute(value, ("ta", "gx"), perm)

    no_x = lambda v: jnp.concatenate([v[:1], v[2:]])
    left = send(links[:, :, :2, :, :, -1].reshape(48, slices, LANES), 0, 1)
    right = send(no_x(links[:, :, :2, :, :, 0]).reshape(36, slices, LANES), 0, -1)
    before = send(links[:, :, :, :, -1].reshape(72, 2, LANES), 1, 0)
    after = send(links[1:, :, :, :, 0].reshape(54, 2, LANES), -1, 0)
    corner_x = send(links[1, :, :, :, 0, -1].reshape(18, 1, LANES), -1, 1)
    corner_t = send(links[0, :, :, :, -1, 0].reshape(18, 1, LANES), 1, -1)

    split = LANES // devices
    rows = 2 * slices
    flowed, packed = pl.pallas_call(
        lambda *refs: flow_kernel(slices, split, *refs),
        out_shape=(
            jax.ShapeDtypeStruct((72, rows, LANES), jnp.float32),
            jax.ShapeDtypeStruct((36, devices, rows * split), jnp.float32),
        ),
        in_specs=[vmem] * 7,
        out_specs=(vmem, vmem),
        scratch_shapes=[
            pltpu.VMEM((72, 4, TOP + slices + 8, LANES), jnp.float32),
            pltpu.VMEM((72, 8, LANES), jnp.float32),
            pltpu.VMEM((72, 2, slices, LANES), jnp.float32),
            pltpu.VMEM((rows * split, LANES), jnp.float32),
        ],
        compiler_params=pltpu.CompilerParams(vmem_limit_bytes=40 * 2**20),
        name="flow",
    )(links.reshape(72, rows, LANES), left, right, before, after, corner_x, corner_t)

    fields = lax.all_to_all(packed, ("ta", "gx"), 1, 1, tiled=True)
    repeats = LANES // (rows * split)
    fields = fields.reshape(36, nta, ngx, rows * split)
    if repeats > 1:
        fields = jnp.tile(fields, (1, 1, 1, repeats))
    entries = pl.pallas_call(
        lambda *refs: loop_kernel(nta, 2 * split, *refs),
        out_shape=jax.ShapeDtypeStruct((LEVELS, TMAX, LANES), jnp.float32),
        in_specs=[vmem],
        out_specs=vmem,
        scratch_shapes=[
            pltpu.VMEM((TMAX, 18, nta * (ngx // 8), 8, LANES), jnp.float32),
            pltpu.VMEM((LEVELS, 18, nta, ngx, LANES), jnp.float32),
            pltpu.VMEM((LEVELS, 18, nta, ngx, LANES), jnp.float32),
            pltpu.VMEM((8, LANES), jnp.float32),
        ],
        compiler_params=pltpu.CompilerParams(vmem_limit_bytes=40 * 2**20),
        name="loops",
    )(fields)
    volume = 3.0 * slices * nta * 2 * ngx * LANES
    table = lax.psum(jnp.sum(entries, axis=2), ("ta", "gx")) / (volume * repeats)
    return flowed.reshape(links.shape), table


def solution(mesh):
    spec = P(None, None, None, None, "ta", "gx", None)
    return jax.shard_map(body, mesh=mesh, in_specs=(spec,), out_specs=(spec, P()), check_vma=False)
```

profile of v0, /device:TPU:0, one launch (start us, length us, event | category | flops | bytes accessed | tf_op | source)
XLA Modules:
  0.0 117.6 jit_solution(2335767394835287308)
XLA Ops:
  0.6 0.0 copy-start
  0.6 1.6 %slice.30 = f32[4,2,2,3,16,1,128]{6,5,4,3,2,1,0:T(1,128)S(1)} slice(f32[4,2,3,3,16,2,128]{6,5,4,3,2,1,0:T(2,128)} %param.1), slice={[0:4], [0:2], [0:2], [0:3], [0:16], [1:2], [0:128]} | slice | bytes 786432 | tf_op jit(solution)/shard_map/slice | solution.py:358
  2.3 3.0 %collective-permute-start = (f32[48,16,128]{2,1,0:T(8,128)S(1)}, f32[48,16,128]{2,1,0:T(8,128)S(1)}, u32[]{:S(2)}, u32[]{:S(2)}) collective-permute-start(f32[48,16,128]{2,1,0:T(8,128)S(1)} %bitcast.18), channel_id=1, source_target_pairs={{0,1},{1,2},{2,3},{3,4},{4,5},{5,6},{6,7},{7,0},{8,9},{9,10},{10,1... | collective-permute-start | bytes 1179656 | tf_op jit(solution)/shard_map/ppermute | solution.py:355
  5.3 1.0 slice.31
  6.3 1.1 slice.33
  7.5 3.1 %collective-permute-start.1 = (f32[36,16,128]{2,1,0:T(8,128)S(1)}, f32[36,16,128]{2,1,0:T(8,128)S(1)}, u32[]{:S(2)}, u32[]{:S(2)}) collective-permute-start(f32[36,16,128]{2,1,0:T(8,128)S(1)} %bitcast.20), channel_id=1, source_target_pairs={{0,7},{1,0},{2,1},{3,2},{4,3},{5,4},{6,5},{7,6},{8,15},{9,8},{10,9... | collective-permute-start | bytes 884744 | tf_op jit(solution)/shard_map/ppermute | solution.py:355
  10.6 0.0 copy-done
  10.6 0.7 collective-permute-start.3
  11.4 0.1 collective-permute-start.2
  11.5 0.1 collective-permute-start.4
  11.5 8.6 %collective-permute-done.4.refs_5_ = f32[18,1,128]{2,1,0:T(1,128)S(1)} collective-permute-done((f32[18,1,128]{2,1,0:T(1,128)S(1)}, f32[18,1,128]{2,1,0:T(1,128)S(1)}, u32[]{:S(2)}, u32[]{:S(2)}) %collective-permute-start.4) | collective-permute-done | bytes 9248 | tf_op jit(solution)/shard_map/ppermute | solution.py:355
  20.2 5.9 %collective-permute-start.5 = (f32[18,1,128]{2,1,0:T(1,128)S(1)}, f32[18,1,128]{2,1,0:T(1,128)S(1)}, u32[]{:S(2)}, u32[]{:S(2)}) collective-permute-start(f32[18,1,128]{2,1,0:T(1,128)S(1)} %bitcast.23), channel_id=1, source_target_pairs={{0,15},{1,8},{2,9},{3,10},{4,11},{5,12},{6,13},{7,14},{8,23},{9,16... | collective-permute-start | bytes 27656 | tf_op jit(solution)/shard_map/ppermute | solution.py:355
  26.1 1.4 %collective-permute-done.5.refs_6_ = f32[18,1,128]{2,1,0:T(1,128)S(1)} collective-permute-done((f32[18,1,128]{2,1,0:T(1,128)S(1)}, f32[18,1,128]{2,1,0:T(1,128)S(1)}, u32[]{:S(2)}, u32[]{:S(2)}) %collective-permute-start.5) | collective-permute-done | bytes 9248 | tf_op jit(solution)/shard_map/ppermute | solution.py:355
  27.4 0.0 collective-permute-done.3.refs_4_
  27.5 0.0 collective-permute-done.2.refs_3_
  27.5 0.0 collective-permute-done.1.refs_2_
  27.5 0.0 collective-permute-done.refs_1_
  27.5 11.4 %flow.1 = (f32[72,32,128]{2,1,0:T(8,128)}, f32[36,32,128]{2,1,0:T(8,128)S(1)}) custom-call(f32[72,32,128]{2,1,0:T(8,128)S(1)} %bitcast.15, f32[48,16,128]{2,1,0:T(8,128)S(1)} %collective-permute-done.refs_1_, f32[36,16,128]{2,1,0:T(8,128)S(1)} %collective-permute-done.1.refs_2_, f32[72,2,128]{2,1,0:T(2,128)S(1)} %collective-permute-done.2.refs_3_, ...), custom_call_target="tpu_custom_call" | custom-call | tf_op jit(solution)/shard_map/flow/pallas_call | solution.py:367
  38.9 0.3 copy.5
  39.2 24.1 %all_to_all.5 = f32[36,32,128]{2,0,1:T(8,128)S(1)} all-to-all(f32[36,32,128]{2,0,1:T(8,128)S(1)} %copy.5), channel_id=1, replica_groups=mesh['ta'=4,'gx'=8] {'ta','gx'}, dimensions={1} | all-to-all | bytes 1179648 | tf_op jit(solution)/shard_map/all_to_all | solution.py:385
  63.3 0.1 copy.9
  63.4 15.2 %loops.1 = f32[5,8,128]{2,1,0:T(8,128)S(1)} custom-call(f32[36,4,8,128]{3,2,1,0:T(8,128)S(1)} %bitcast.16), custom_call_target="tpu_custom_call" | custom-call | tf_op jit(solution)/shard_map/loops/pallas_call | solution.py:390
  78.6 0.1 reduce_sum.9
  78.7 38.3 %psum.7 = f32[5,8]{1,0:T(8,128)S(1)} all-reduce(f32[5,8]{1,0:T(8,128)S(1)} %reduce_sum.9), channel_id=1, replica_groups=mesh['ta'=4,'gx'=8] {'ta','gx'}, use_global_device_ids=true, to_apply=%region_1.0 | all-reduce | flops 40 | bytes 320 | tf_op jit(solution)/shard_map/psum | solution.py:405
  117.0 0.6 broadcast_multiply_fusion
  (4 shorter events, 0.1 us)
Async XLA Ops:
  0.6 9.9 %copy-start = (f32[4,2,3,3,16,2,128]{6,5,4,3,2,1,0:T(2,128)S(1)}, f32[4,2,3,3,16,2,128]{6,5,4,3,2,1,0:T(2,128)}, u32[]{:S(2)}) copy-start(f32[4,2,3,3,16,2,128]{6,5,4,3,2,1,0:T(2,128)} %param.1) | copy-start | bytes 3538948
  2.3 25.2 %collective-permute-start = (f32[48,16,128]{2,1,0:T(8,128)S(1)}, f32[48,16,128]{2,1,0:T(8,128)S(1)}, u32[]{:S(2)}, u32[]{:S(2)}) collective-permute-start(f32[48,16,128]{2,1,0:T(8,128)S(1)} %bitcast.18), channel_id=1, source_target_pairs={{0,1},{1,2},{2,3},{3,4},{4,5},{5,6},{6,7},{7,0},{8,9},{9,10},{10,1... | collective-permute-start | bytes 1179656 | tf_op jit(solution)/shard_map/ppermute | solution.py:355
  7.5 20.0 %collective-permute-start.1 = (f32[36,16,128]{2,1,0:T(8,128)S(1)}, f32[36,16,128]{2,1,0:T(8,128)S(1)}, u32[]{:S(2)}, u32[]{:S(2)}) collective-permute-start(f32[36,16,128]{2,1,0:T(8,128)S(1)} %bitcast.20), channel_id=1, source_target_pairs={{0,7},{1,0},{2,1},{3,2},{4,3},{5,4},{6,5},{7,6},{8,15},{9,8},{10,9... | collective-permute-start | bytes 884744 | tf_op jit(solution)/shard_map/ppermute | solution.py:355
  10.6 16.9 %collective-permute-start.3 = (f32[54,2,128]{2,1,0:T(2,128)S(1)}, f32[54,2,128]{2,1,0:T(2,128)S(1)}, u32[]{:S(2)}, u32[]{:S(2)}) collective-permute-start(f32[54,2,128]{2,1,0:T(2,128)S(1)} %bitcast.22), channel_id=1, source_target_pairs={{0,24},{1,25},{2,26},{3,27},{4,28},{5,29},{6,30},{7,31},{8,0},{9,1... | collective-permute-start | bytes 165896 | tf_op jit(solution)/shard_map/ppermute | solution.py:355
  11.4 16.1 %collective-permute-start.2 = (f32[72,2,128]{2,1,0:T(2,128)S(1)}, f32[72,2,128]{2,1,0:T(2,128)S(1)}, u32[]{:S(2)}, u32[]{:S(2)}) collective-permute-start(f32[72,2,128]{2,1,0:T(2,128)S(1)} %bitcast.21), channel_id=1, source_target_pairs={{0,8},{1,9},{2,10},{3,11},{4,12},{5,13},{6,14},{7,15},{8,16},{9,17... | collective-permute-start | bytes 221192 | tf_op jit(solution)/shard_map/ppermute | solution.py:355
  11.5 8.7 %collective-permute-start.4 = (f32[18,1,128]{2,1,0:T(1,128)S(1)}, f32[18,1,128]{2,1,0:T(1,128)S(1)}, u32[]{:S(2)}, u32[]{:S(2)}) collective-permute-start(f32[18,1,128]{2,1,0:T(1,128)S(1)} %bitcast.24), channel_id=1, source_target_pairs={{0,25},{1,26},{2,27},{3,28},{4,29},{5,30},{6,31},{7,24},{8,1},{9,2... | collective-permute-start | bytes 27656 | tf_op jit(solution)/shard_map/ppermute | solution.py:355
  20.2 7.3 %collective-permute-start.5 = (f32[18,1,128]{2,1,0:T(1,128)S(1)}, f32[18,1,128]{2,1,0:T(1,128)S(1)}, u32[]{:S(2)}, u32[]{:S(2)}) collective-permute-start(f32[18,1,128]{2,1,0:T(1,128)S(1)} %bitcast.23), channel_id=1, source_target_pairs={{0,15},{1,8},{2,9},{3,10},{4,11},{5,12},{6,13},{7,14},{8,23},{9,16... | collective-permute-start | bytes 27656 | tf_op jit(solution)/shard_map/ppermute | solution.py:355
where the time goes:
time: 118 us
  blocking collectives  62.3 us (53%)
  Pallas kernels  26.6 us (23%)
  starting transfers between devices  12.8 us (11%)
  waiting for transfers between devices  10 us (8%)
  local copies, waits for them, and re-layouts  4.33 us (4%)
    psum x1, blocking collectives, body(): lax.psum(jnp.sum(entries, axis=2), ('ta', 'gx')) / (volume * repeats)  38.3 us
    all_to_all x1, blocking collectives, body(): fields = lax.all_to_all(packed, ('ta', 'gx'), 1, 1, tiled=True)  24.1 us
    pallas_call x1, Pallas kernels, body(): pl.pallas_call(lambda *refs: loop_kernel(nta, 2 * split, *refs), out_shap...  15.2 us
    ppermute x6, starting transfers between devices, send(): return lax.ppermute(value, ('ta', 'gx'), perm)  12.8 us
    pallas_call x1, Pallas kernels, body(): pl.pallas_call(lambda *refs: flow_kernel(slices, split, *refs), out_shape...  11.4 us
    ppermute x6, waiting for transfers between devices, send(): return lax.ppermute(value, ('ta', 'gx'), perm)  10 us
  transfers between devices with their start and end apart: 6, of which 2 were waited for; matrix products, arithmetic and copies ran while one was open for 2% of the time, Pallas kernels for 0%

commit v1 on v0

--- a/solution.py
+++ b/solution.py
@@ -252,7 +252,7 @@
     lax.fori_loop(0, 36 // split, pack, 0)
 
 
-def loop_kernel(blocks, per_slice, fields, out, early, lines, ahead, line_ahead):
+def loop_kernel(blocks, per_slice, fields, out, early, lines, ahead):
     groups = fields.shape[2]
     lane_all = lax.broadcasted_iota(jnp.int32, (groups, LANES), 1)
     odd = (lane_all & 1) == 1
@@ -334,11 +334,123 @@
             return tuple(new)
 
         totals = lax.fori_loop(0, cells, cell, (jnp.zeros((8, LANES), jnp.float32),) * TMAX)
-        for s in range(TMAX):
-            out[k, pl.ds(s, 1), :] = jnp.sum(totals[s], axis=0, keepdims=True)
-        return 0
-
+        block = jnp.concatenate([jnp.sum(t, axis=0, keepdims=True) for t in totals], axis=0)
+        out[...] = jnp.where(lane == k, jnp.sum(block, axis=1, keepdims=True), out[...])
+        return 0
+
+    out[...] = jnp.zeros((TMAX, LANES), jnp.float32)
     lax.fori_loop(0, LEVELS, level, 0)
+
+
+MESH = pl.DeviceIdType.MESH
+
+
+def halo_kernel(nta, ngx, slices, links, left, right, before, after, corner_x, corner_t, send_sems, recv_sems):
+    ta, gx = lax.axis_index("ta"), lax.axis_index("gx")
+    there = lambda dt, dx: (lax.rem(ta + dt + nta, nta), lax.rem(gx + dx + ngx, ngx))
+    barrier = pltpu.get_barrier_semaphore()
+    steps = ((0, 1), (0, -1), (1, 0), (-1, 0), (-1, 1), (1, -1))
+    for step in steps:
+        pl.semaphore_signal(barrier, inc=1, device_id=there(*step), device_id_type=MESH)
+    pl.semaphore_wait(barrier, len(steps))
+    last = slices - 1
+    moves = (
+        (links.at[:, 0:6, :, 1], left, (0, 1)),
+        (links.at[0:2, 0:6, :, 0], right.at[0:2], (0, -1)),
+        (links.at[4:8, 0:6, :, 0], right.at[2:6], (0, -1)),
+        (links.at[:, :, last], before, (1, 0)),
+        (links.at[2:8, :, 0], after, (-1, 0)),
+        (links.at[2:4, :, 0, 1], corner_x, (-1, 1)),
+        (links.at[0:2, :, last, 0], corner_t, (1, -1)),
+    )
+    copies = [
+        pltpu.make_async_remote_copy(
+            src_ref=source,
+            dst_ref=target,
+            send_sem=send_sems.at[n],
+            recv_sem=recv_sems.at[n],
+            device_id=there(*step),
+            device_id_type=MESH,
+        )
+        for n, (source, target, step) in enumerate(moves)
+    ]
+    for copy in copies:
+        copy.start()
+    for copy in copies:
+        copy.wait()
+
+
+def meet_all(ngx, devices, me):
+    barrier = pltpu.get_barrier_semaphore()
+
+    def greet(k, _):
+        other = lax.rem(me + k, devices)
+        pl.semaphore_signal(barrier, inc=1, device_id=(other // ngx, lax.rem(other, ngx)), device_id_type=MESH)
+        return 0
+
+    lax.fori_loop(1, devices, greet, 0)
+    pl.semaphore_wait(barrier, devices - 1)
+
+
+def exchange_kernel(nta, ngx, packed, fields, send_sems, recv_sems, own_sem):
+    devices = nta * ngx
+    me = lax.axis_index("ta") * ngx + lax.axis_index("gx")
+    meet_all(ngx, devices, me)
+
+    def move(k):
+        other = lax.rem(me + k, devices)
+        return pltpu.make_async_remote_copy(
+            src_ref=packed.at[:, other],
+            dst_ref=fields.at[:, me],
+            send_sem=send_sems.at[k],
+            recv_sem=recv_sems.at[k],
+            device_id=(other // ngx, lax.rem(other, ngx)),
+            device_id_type=MESH,
+        )
+
+    def start(k, _):
+        move(k).start()
+        return 0
+
+    def wait(k, _):
+        move(k).wait()
+        return 0
+
+    lax.fori_loop(1, devices, start, 0)
+    own = pltpu.make_async_copy(packed.at[:, me], fields.at[:, me], own_sem)
+    own.start()
+    own.wait()
+    lax.fori_loop(1, devices, wait, 0)
+
+
+def total_kernel(nta, ngx, scale, part, total, slots, send_sems, recv_sems):
+    devices = nta * ngx
+    me = lax.axis_index("ta") * ngx + lax.axis_index("gx")
+    meet_all(ngx, devices, me)
+
+    def move(k):
+        other = lax.rem(me + k, devices)
+        return pltpu.make_async_remote_copy(
+            src_ref=part,
+            dst_ref=slots.at[me],
+            send_sem=send_sems.at[k],
+            recv_sem=recv_sems.at[k],
+            device_id=(other // ngx, lax.rem(other, ngx)),
+            device_id_type=MESH,
+        )
+
+    def start(k, _):
+        move(k).start()
+        return 0
+
+    def wait(k, _):
+        move(k).wait()
+        return 0
+
+    lax.fori_loop(1, devices, start, 0)
+    slots[me] = part[...]
+    lax.fori_loop(1, devices, wait, 0)
+    total[...] = jnp.sum(slots[...], axis=0) * scale
 
 
 def body(links):
@@ -346,64 +458,85 @@
     devices = nta * ngx
     slices = links.shape[4]
     vmem = pl.BlockSpec(memory_space=pltpu.VMEM)
-
-    def send(value, dt, dx):
-        perm = []
-        for i in range(nta):
-            for j in range(ngx):
-                perm.append((i * ngx + j, ((i + dt) % nta) * ngx + (j + dx) % ngx))
-        return lax.ppermute(value, ("ta", "gx"), perm)
-
-    no_x = lambda v: jnp.concatenate([v[:1], v[2:]])
-    left = send(links[:, :, :2, :, :, -1].reshape(48, slices, LANES), 0, 1)
-    right = send(no_x(links[:, :, :2, :, :, 0]).reshape(36, slices, LANES), 0, -1)
-    before = send(links[:, :, :, :, -1].reshape(72, 2, LANES), 1, 0)
-    after = send(links[1:, :, :, :, 0].reshape(54, 2, LANES), -1, 0)
-    corner_x = send(links[1, :, :, :, 0, -1].reshape(18, 1, LANES), -1, 1)
-    corner_t = send(links[0, :, :, :, -1, 0].reshape(18, 1, LANES), 1, -1)
+    anywhere = pl.BlockSpec(memory_space=pl.ANY)
+    array = lambda *shape: jax.ShapeDtypeStruct(shape, jnp.float32)
+    sems = pltpu.SemaphoreType.DMA
+    remote = lambda n: pltpu.CompilerParams(collective_id=n, has_side_effects=True)
+
+    halos = pl.pallas_call(
+        lambda *refs: halo_kernel(nta, ngx, slices, *refs),
+        out_shape=(
+            array(8, 6, slices, 1, LANES),
+            array(6, 6, slices, 1, LANES),
+            array(8, 9, 2, 1, LANES),
+            array(6, 9, 2, 1, LANES),
+            array(2, 9, 1, LANES),
+            array(2, 9, 1, LANES),
+        ),
+        in_specs=[anywhere],
+        out_specs=(vmem,) * 6,
+        scratch_shapes=[sems((7,)), sems((7,))],
+        compiler_params=remote(0),
+        name="halos",
+    )(links.reshape(8, 9, slices, 2, 1, LANES))
+    shapes = ((48, slices, LANES), (36, slices, LANES), (72, 2, LANES), (54, 2, LANES), (18, 1, LANES), (18, 1, LANES))
+    halos = [v.reshape(shape) for v, shape in zip(halos, shapes)]
 
     split = LANES // devices
     rows = 2 * slices
+    width = rows * split
     flowed, packed = pl.pallas_call(
         lambda *refs: flow_kernel(slices, split, *refs),
-        out_shape=(
-            jax.ShapeDtypeStruct((72, rows, LANES), jnp.float32),
-            jax.ShapeDtypeStruct((36, devices, rows * split), jnp.float32),
-        ),
+        out_shape=(array(72, rows, LANES), array(36, devices, width)),
         in_specs=[vmem] * 7,
         out_specs=(vmem, vmem),
         scratch_shapes=[
             pltpu.VMEM((72, 4, TOP + slices + 8, LANES), jnp.float32),
             pltpu.VMEM((72, 8, LANES), jnp.float32),
             pltpu.VMEM((72, 2, slices, LANES), jnp.float32),
-            pltpu.VMEM((rows * split, LANES), jnp.float32),
+            pltpu.VMEM((width, LANES), jnp.float32),
         ],
         compiler_params=pltpu.CompilerParams(vmem_limit_bytes=40 * 2**20),
         name="flow",
-    )(links.reshape(72, rows, LANES), left, right, before, after, corner_x, corner_t)
-
-    fields = lax.all_to_all(packed, ("ta", "gx"), 1, 1, tiled=True)
-    repeats = LANES // (rows * split)
-    fields = fields.reshape(36, nta, ngx, rows * split)
+    )(links.reshape(72, rows, LANES), *halos)
+
+    fields = pl.pallas_call(
+        lambda *refs: exchange_kernel(nta, ngx, *refs),
+        out_shape=array(36, devices, 1, width),
+        in_specs=[vmem],
+        out_specs=vmem,
+        scratch_shapes=[sems((devices,)), sems((devices,)), sems],
+        compiler_params=remote(1),
+        name="exchange",
+    )(packed.reshape(36, devices, 1, width))
+    repeats = LANES // width
+    fields = fields.reshape(36, nta, ngx, width)
     if repeats > 1:
         fields = jnp.tile(fields, (1, 1, 1, repeats))
-    entries = pl.pallas_call(
+    part = pl.pallas_call(
         lambda *refs: loop_kernel(nta, 2 * split, *refs),
-        out_shape=jax.ShapeDtypeStruct((LEVELS, TMAX, LANES), jnp.float32),
+        out_shape=array(TMAX, LANES),
         in_specs=[vmem],
         out_specs=vmem,
         scratch_shapes=[
             pltpu.VMEM((TMAX, 18, nta * (ngx // 8), 8, LANES), jnp.float32),
             pltpu.VMEM((LEVELS, 18, nta, ngx, LANES), jnp.float32),
             pltpu.VMEM((LEVELS, 18, nta, ngx, LANES), jnp.float32),
-            pltpu.VMEM((8, LANES), jnp.float32),
         ],
         compiler_params=pltpu.CompilerParams(vmem_limit_bytes=40 * 2**20),
         name="loops",
     )(fields)
-    volume = 3.0 * slices * nta * 2 * ngx * LANES
-    table = lax.psum(jnp.sum(entries, axis=2), ("ta", "gx")) / (volume * repeats)
-    return flowed.reshape(links.shape), table
+    scale = 1.0 / (3.0 * slices * nta * 2 * ngx * LANES * repeats)
+    total = pl.pallas_call(
+        lambda *refs: total_kernel(nta, ngx, scale, *refs),
+        out_shape=array(TMAX, LANES),
+        in_specs=[vmem],
+        out_specs=vmem,
+        scratch_shapes=[pltpu.VMEM((devices, TMAX, LANES), jnp.float32), sems((devices,)), sems((devices,))],
+        compiler_params=remote(2),
+        name="total",
+    )(part)
+    return flowed.reshape(links.shape), total[:, :LEVELS].T
 
 
 def solution(mesh):

time: 118 us -> 90.5 us (0.77)
  blocking collectives: 62.3 us -> 0 us
  Pallas kernels: 26.6 us -> 80.4 us
  starting transfers between devices: 12.8 us -> 0 us
  waiting for transfers between devices: 10 us -> 0 us
  local copies, waits for them, and re-layouts: 4.33 us -> 8.85 us
    pallas_call x0 -> x3, Pallas kernels: none -> 53.4 us  [the longest x1 22.4 us: body(): pl.pallas_call(lambda *refs: halo_kernel(nta, ngx, slices, *refs), out_sh...]
    psum x1 -> x0, blocking collectives: 38.3 us -> none  [body(): lax.psum(jnp.sum(entries, axis=2), ('ta', 'gx')) / (volume * repeats)]
    all_to_all x1 -> x0, blocking collectives: 24.1 us -> none  [body(): fields = lax.all_to_all(packed, ('ta', 'gx'), 1, 1, tiled=True)]
    ppermute x6 -> x0, starting transfers between devices: 12.8 us -> none  [send(): return lax.ppermute(value, ('ta', 'gx'), perm)]
    ppermute x6 -> x0, waiting for transfers between devices: 10 us -> none  [send(): return lax.ppermute(value, ('ta', 'gx'), perm)]
    unnamed x2 -> x21, local copies, waits for them, and re-layouts: 0.01 us -> 8.18 us
    slice x6 -> x0, local copies, waits for them, and re-layouts: 3.86 us -> none  [the longest x2 2.14 us: body(): no_x = lambda v: jnp.concatenate([v[:1], v[2:]])]
  transfers between devices with their start and end apart: 6 -> 0, of which waited for: 2 -> 0; matrix products, arithmetic and copies ran while one was open for 2% -> 0% of each run, Pallas kernels for 0% -> 0%
where the time goes in v1:
time: 90.5 us; the launch traced here: 89.9 us
  Pallas kernels  80.4 us (89%)
  local copies, waits for them, and re-layouts  8.85 us (10%)
    pallas_call x1, Pallas kernels, body(): pl.pallas_call(lambda *refs: halo_kernel(nta, ngx, slices, *refs), out_sh...  22.4 us
    pallas_call x1, Pallas kernels, body(): pl.pallas_call(lambda *refs: exchange_kernel(nta, ngx, *refs), out_shape=...  20.5 us
    pallas_call x1, Pallas kernels, body(): pl.pallas_call(lambda *refs: loop_kernel(nta, 2 * split, *refs), out_shap...  15.6 us
    pallas_call x1, Pallas kernels, body(): pl.pallas_call(lambda *refs: flow_kernel(slices, split, *refs), out_shape...  11.4 us
    pallas_call x1, Pallas kernels, body(): pl.pallas_call(lambda *refs: total_kernel(nta, ngx, scale, *refs), out_sh...  10.5 us
    unnamed x21, local copies, waits for them, and re-layouts  8.18 us

profile of v1, /device:TPU:0, one launch (start us, length us, event | category | flops | bytes accessed | tf_op | source)
XLA Modules:
  0.0 89.9 jit_solution(1712248922533752889)
XLA Ops:
  0.6 0.0 copy-start
  0.6 22.4 %halos.1 = (f32[8,6,16,1,128]{4,3,2,1,0:T(1,128)}, f32[6,6,16,1,128]{4,3,2,1,0:T(1,128)}, f32[8,9,2,1,128]{4,3,2,1,0:T(1,128)}, f32[6,9,2,1,128]{4,3,2,1,0:T(1,1...) custom-call(f32[8,9,16,2,1,128]{5,4,3,2,1,0:T(1,128)} %bitcast.13), custom_call_target="tpu_custom_call" | custom-call | tf_op jit(solution)/shard_map/halos/pallas_call | solution.py:466
  23.1 0.0 copy-done
  23.1 0.0 copy-start.3
  23.1 1.0 %copy-done.3 = f32[8,6,16,1,128]{4,3,2,1,0:T(1,128)S(1)} copy-done((f32[8,6,16,1,128]{4,3,2,1,0:T(1,128)S(1)}, f32[8,6,16,1,128]{4,3,2,1,0:T(1,128)}, u32[]{:S(2)}) %copy-start.3) | copy-done | bytes 393240
  24.1 0.0 copy-start.4
  24.1 1.0 %copy-done.4 = f32[6,6,16,1,128]{4,3,2,1,0:T(1,128)S(1)} copy-done((f32[6,6,16,1,128]{4,3,2,1,0:T(1,128)S(1)}, f32[6,6,16,1,128]{4,3,2,1,0:T(1,128)}, u32[]{:S(2)}) %copy-start.4) | copy-done | bytes 294936
  25.0 0.0 copy-start.5
  25.0 0.9 copy-done.5
  25.9 0.0 copy-start.6
  25.9 0.8 copy-done.6
  26.7 0.0 copy-start.8
  26.7 0.7 copy-done.8
  27.4 0.0 copy-start.9
  27.4 0.7 copy-done.9
  28.1 11.4 %flow.1 = (f32[72,32,128]{2,1,0:T(8,128)}, f32[36,32,128]{2,1,0:T(8,128)S(1)}) custom-call(f32[72,32,128]{2,1,0:T(8,128)S(1)} %bitcast.14, f32[48,16,128]{2,1,0:T(8,128)S(1)} %bitcast.17, f32[36,16,128]{2,1,0:T(8,128)S(1)} %bitcast.18, f32[72,2,128]{2,1,0:T(2,128)S(1)} %bitcast.19, f32[54,2,128]{2,1,0:T(2,128)S(1)} %bitcast.20, f32[18,1,128]{2,1,0:T(1,128)S(1)} %bitcast.21, ...), custom_call_target="tpu_custom_call" | custom-call | tf_op jit(solution)/shard_map/flow/pallas_call | solution.py:488
  39.5 0.0 copy-start.2
  39.5 0.8 copy-done.2
  40.3 20.5 %exchange.1 = f32[36,32,1,128]{3,2,1,0:T(1,128)} custom-call(f32[36,32,1,128]{3,2,1,0:T(1,128)} %bitcast.16), custom_call_target="tpu_custom_call" | custom-call | tf_op jit(solution)/shard_map/exchange/pallas_call | solution.py:503
  60.8 0.0 copy-start.1
  60.8 1.1 %copy-done.1 = f32[36,32,1,128]{3,2,1,0:T(1,128)S(1)} copy-done((f32[36,32,1,128]{3,2,1,0:T(1,128)S(1)}, f32[36,32,1,128]{3,2,1,0:T(1,128)}, u32[]{:S(2)}) %copy-start.1) | copy-done | bytes 589848
  61.9 15.6 %loops.1.refs_0_ = f32[8,128]{1,0:T(8,128)S(1)} custom-call(f32[36,4,8,128]{3,2,1,0:T(8,128)S(1)} %bitcast.15), custom_call_target="tpu_custom_call" | custom-call | tf_op jit(solution)/shard_map/loops/pallas_call | solution.py:516
  77.5 0.0 copy-start.7
  77.5 0.6 copy-done.7
  78.1 10.5 %total.1 = f32[8,128]{1,0:T(8,128)} custom-call(f32[8,128]{1,0:T(8,128)} %copy-done.7), custom_call_target="tpu_custom_call" | custom-call | tf_op jit(solution)/shard_map/total/pallas_call | solution.py:530
  88.6 0.7 slice_bitcast_fusion
  89.3 0.7 copy.3
Async XLA Ops:
  0.6 22.4 %copy-start = (f32[4,2,3,3,16,2,128]{6,5,4,3,2,1,0:T(2,128)S(1)}, f32[4,2,3,3,16,2,128]{6,5,4,3,2,1,0:T(2,128)}, u32[]{:S(2)}) copy-start(f32[4,2,3,3,16,2,128]{6,5,4,3,2,1,0:T(2,128)} %param.1) | copy-start | bytes 3538948
  23.1 1.0 %copy-start.3 = (f32[8,6,16,1,128]{4,3,2,1,0:T(1,128)S(1)}, f32[8,6,16,1,128]{4,3,2,1,0:T(1,128)}, u32[]{:S(2)}) copy-start(f32[8,6,16,1,128]{4,3,2,1,0:T(1,128)} %get-tuple-element.10) | copy-start | bytes 1179652
  24.1 1.0 %copy-start.4 = (f32[6,6,16,1,128]{4,3,2,1,0:T(1,128)S(1)}, f32[6,6,16,1,128]{4,3,2,1,0:T(1,128)}, u32[]{:S(2)}) copy-start(f32[6,6,16,1,128]{4,3,2,1,0:T(1,128)} %get-tuple-element.11) | copy-start | bytes 884740
  25.0 0.9 copy-start.5
  25.9 0.8 copy-start.6
  26.7 0.7 copy-start.8
  27.4 0.7 copy-start.9
  39.5 0.8 copy-start.2
  60.8 1.1 %copy-start.1 = (f32[36,32,1,128]{3,2,1,0:T(1,128)S(1)}, f32[36,32,1,128]{3,2,1,0:T(1,128)}, u32[]{:S(2)}) copy-start(f32[36,32,1,128]{3,2,1,0:T(1,128)} %exchange.1) | copy-start | bytes 1769476
  77.5 0.6 copy-start.7

commit v2 on v1

--- a/solution.py
+++ b/solution.py
@@ -246,17 +246,22 @@
                     turn[pl.ds(8 * 2 * split * h + 2 * k + p, 8, stride=2 * split), :] = mixed
         turned = jnp.transpose(turn[...])
         for c in range(split):
-            packed[split * g + c] = turned[width * c : width * c + width, :]
-        return 0
-
-    lax.fori_loop(0, 36 // split, pack, 0)
-
-
-def loop_kernel(blocks, per_slice, fields, out, early, lines, ahead):
+            packed[pl.ds(split * g + c, width, stride=36), :] = turned[width * c : width * c + width, :]
+        return 0
+
+    for g in range(36 // split):
+        pack(g, 0)
+
+
+def loop_kernel(blocks, per_slice, arrived, out, fields, early, lines, ahead):
     groups = fields.shape[2]
+    for b in range(blocks):
+        for c in range(36):
+            fields[c, b] = arrived[pl.ds(36 * groups * b + c, groups, stride=36), :]
     lane_all = lax.broadcasted_iota(jnp.int32, (groups, LANES), 1)
     odd = (lane_all & 1) == 1
     lane = lax.broadcasted_iota(jnp.int32, (8, LANES), 1)
+    row = lax.broadcasted_iota(jnp.int32, (8, LANES), 0)
     slices = 16
 
     def forward_x(v, distance):
@@ -335,7 +340,8 @@
 
         totals = lax.fori_loop(0, cells, cell, (jnp.zeros((8, LANES), jnp.float32),) * TMAX)
         block = jnp.concatenate([jnp.sum(t, axis=0, keepdims=True) for t in totals], axis=0)
-        out[...] = jnp.where(lane == k, jnp.sum(block, axis=1, keepdims=True), out[...])
+        spread = jnp.where(lane == row, jnp.sum(block, axis=1, keepdims=True), 0.0)
+        out[...] = jnp.where(row == k, jnp.sum(spread, axis=0, keepdims=True), out[...])
         return 0
 
     out[...] = jnp.zeros((TMAX, LANES), jnp.float32)
@@ -345,19 +351,32 @@
 MESH = pl.DeviceIdType.MESH
 
 
-def halo_kernel(nta, ngx, slices, links, left, right, before, after, corner_x, corner_t, send_sems, recv_sems):
+def halo_kernel(nta, ngx, slices, links, left, right, before, after, corner_x, corner_t, last_plane, first_plane, local_sems, send_sems, recv_sems):
     ta, gx = lax.axis_index("ta"), lax.axis_index("gx")
     there = lambda dt, dx: (lax.rem(ta + dt + nta, nta), lax.rem(gx + dx + ngx, ngx))
+    local = [
+        pltpu.make_async_copy(source, target, local_sems.at[n])
+        for n, (source, target) in enumerate(
+            (
+                (links.at[:, 0:6, :, 1], last_plane),
+                (links.at[0:2, 0:6, :, 0], first_plane.at[0:2]),
+                (links.at[4:8, 0:6, :, 0], first_plane.at[2:6]),
+            )
+        )
+    ]
+    for copy in local:
+        copy.start()
     barrier = pltpu.get_barrier_semaphore()
     steps = ((0, 1), (0, -1), (1, 0), (-1, 0), (-1, 1), (1, -1))
     for step in steps:
         pl.semaphore_signal(barrier, inc=1, device_id=there(*step), device_id_type=MESH)
     pl.semaphore_wait(barrier, len(steps))
     last = slices - 1
+    for copy in local:
+        copy.wait()
     moves = (
-        (links.at[:, 0:6, :, 1], left, (0, 1)),
-        (links.at[0:2, 0:6, :, 0], right.at[0:2], (0, -1)),
-        (links.at[4:8, 0:6, :, 0], right.at[2:6], (0, -1)),
+        (last_plane, left, (0, 1)),
+        (first_plane, right, (0, -1)),
         (links.at[:, :, last], before, (1, 0)),
         (links.at[2:8, :, 0], after, (-1, 0)),
         (links.at[2:4, :, 0, 1], corner_x, (-1, 1)),
@@ -400,8 +419,8 @@
     def move(k):
         other = lax.rem(me + k, devices)
         return pltpu.make_async_remote_copy(
-            src_ref=packed.at[:, other],
-            dst_ref=fields.at[:, me],
+            src_ref=packed.at[other],
+            dst_ref=fields.at[me],
             send_sem=send_sems.at[k],
             recv_sem=recv_sems.at[k],
             device_id=(other // ngx, lax.rem(other, ngx)),
@@ -417,40 +436,56 @@
         return 0
 
     lax.fori_loop(1, devices, start, 0)
-    own = pltpu.make_async_copy(packed.at[:, me], fields.at[:, me], own_sem)
+    own = pltpu.make_async_copy(packed.at[me], fields.at[me], own_sem)
     own.start()
     own.wait()
     lax.fori_loop(1, devices, wait, 0)
 
 
-def total_kernel(nta, ngx, scale, part, total, slots, send_sems, recv_sems):
-    devices = nta * ngx
-    me = lax.axis_index("ta") * ngx + lax.axis_index("gx")
-    meet_all(ngx, devices, me)
-
-    def move(k):
-        other = lax.rem(me + k, devices)
-        return pltpu.make_async_remote_copy(
-            src_ref=part,
-            dst_ref=slots.at[me],
-            send_sem=send_sems.at[k],
-            recv_sem=recv_sems.at[k],
-            device_id=(other // ngx, lax.rem(other, ngx)),
-            device_id_type=MESH,
-        )
-
-    def start(k, _):
-        move(k).start()
-        return 0
-
-    def wait(k, _):
-        move(k).wait()
-        return 0
-
-    lax.fori_loop(1, devices, start, 0)
-    slots[me] = part[...]
-    lax.fori_loop(1, devices, wait, 0)
-    total[...] = jnp.sum(slots[...], axis=0) * scale
+def total_kernel(nta, ngx, scale, part, total, row, slots_x, slots_t, sends_x, recvs_x, sends_t, recvs_t):
+    ta, gx = lax.axis_index("ta"), lax.axis_index("gx")
+    barrier = pltpu.get_barrier_semaphore()
+    in_x = lambda k: (ta, lax.rem(gx + k, ngx))
+    in_t = lambda k: (lax.rem(ta + k, nta), gx)
+
+    def greet(peer):
+        def one(k, _):
+            pl.semaphore_signal(barrier, inc=1, device_id=peer(k), device_id_type=MESH)
+            return 0
+
+        return one
+
+    lax.fori_loop(1, ngx, greet(in_x), 0)
+    lax.fori_loop(1, nta, greet(in_t), 0)
+    pl.semaphore_wait(barrier, ngx + nta - 2)
+
+    def gather(source, slots, mine, count, peer, sends, recvs):
+        def move(k):
+            return pltpu.make_async_remote_copy(
+                src_ref=source,
+                dst_ref=slots.at[mine],
+                send_sem=sends.at[k],
+                recv_sem=recvs.at[k],
+                device_id=peer(k),
+                device_id_type=MESH,
+            )
+
+        def start(k, _):
+            move(k).start()
+            return 0
+
+        def wait(k, _):
+            move(k).wait()
+            return 0
+
+        lax.fori_loop(1, count, start, 0)
+        slots[mine] = source[...]
+        lax.fori_loop(1, count, wait, 0)
+        return jnp.sum(slots[...], axis=0)
+
+    row[...] = gather(part, slots_x, gx, ngx, in_x, sends_x, recvs_x)
+    summed = gather(row, slots_t, ta, nta, in_t, sends_t, recvs_t) * scale
+    total[...] = summed[:LEVELS, :TMAX]
 
 
 def body(links):
@@ -461,7 +496,7 @@
     anywhere = pl.BlockSpec(memory_space=pl.ANY)
     array = lambda *shape: jax.ShapeDtypeStruct(shape, jnp.float32)
     sems = pltpu.SemaphoreType.DMA
-    remote = lambda n: pltpu.CompilerParams(collective_id=n, has_side_effects=True)
+    remote = lambda n: pltpu.CompilerParams(collective_id=n, has_side_effects=True, vmem_limit_bytes=8 * 2**20)
 
     halos = pl.pallas_call(
         lambda *refs: halo_kernel(nta, ngx, slices, *refs),
@@ -475,7 +510,13 @@
         ),
         in_specs=[anywhere],
         out_specs=(vmem,) * 6,
-        scratch_shapes=[sems((7,)), sems((7,))],
+        scratch_shapes=[
+            pltpu.VMEM((8, 6, slices, 1, LANES), jnp.float32),
+            pltpu.VMEM((6, 6, slices, 1, LANES), jnp.float32),
+            sems((3,)),
+            sems((6,)),
+            sems((6,)),
+        ],
         compiler_params=remote(0),
         name="halos",
     )(links.reshape(8, 9, slices, 2, 1, LANES))
@@ -487,7 +528,7 @@
     width = rows * split
     flowed, packed = pl.pallas_call(
         lambda *refs: flow_kernel(slices, split, *refs),
-        out_shape=(array(72, rows, LANES), array(36, devices, width)),
+        out_shape=(array(72, rows, LANES), array(36 * devices, width)),
         in_specs=[vmem] * 7,
         out_specs=(vmem, vmem),
         scratch_shapes=[
@@ -496,47 +537,56 @@
             pltpu.VMEM((72, 2, slices, LANES), jnp.float32),
             pltpu.VMEM((width, LANES), jnp.float32),
         ],
-        compiler_params=pltpu.CompilerParams(vmem_limit_bytes=40 * 2**20),
+        compiler_params=pltpu.CompilerParams(vmem_limit_bytes=24 * 2**20),
         name="flow",
     )(links.reshape(72, rows, LANES), *halos)
 
     fields = pl.pallas_call(
         lambda *refs: exchange_kernel(nta, ngx, *refs),
-        out_shape=array(36, devices, 1, width),
+        out_shape=array(devices, 36, 1, width),
         in_specs=[vmem],
         out_specs=vmem,
         scratch_shapes=[sems((devices,)), sems((devices,)), sems],
         compiler_params=remote(1),
         name="exchange",
-    )(packed.reshape(36, devices, 1, width))
+    )(packed.reshape(devices, 36, 1, width))
     repeats = LANES // width
-    fields = fields.reshape(36, nta, ngx, width)
+    fields = fields.reshape(devices * 36, width)
     if repeats > 1:
-        fields = jnp.tile(fields, (1, 1, 1, repeats))
+        fields = jnp.tile(fields, (1, repeats))
     part = pl.pallas_call(
         lambda *refs: loop_kernel(nta, 2 * split, *refs),
         out_shape=array(TMAX, LANES),
         in_specs=[vmem],
         out_specs=vmem,
         scratch_shapes=[
+            pltpu.VMEM((36, nta, ngx, LANES), jnp.float32),
             pltpu.VMEM((TMAX, 18, nta * (ngx // 8), 8, LANES), jnp.float32),
             pltpu.VMEM((LEVELS, 18, nta, ngx, LANES), jnp.float32),
             pltpu.VMEM((LEVELS, 18, nta, ngx, LANES), jnp.float32),
         ],
-        compiler_params=pltpu.CompilerParams(vmem_limit_bytes=40 * 2**20),
+        compiler_params=pltpu.CompilerParams(vmem_limit_bytes=24 * 2**20),
         name="loops",
     )(fields)
     scale = 1.0 / (3.0 * slices * nta * 2 * ngx * LANES * repeats)
     total = pl.pallas_call(
         lambda *refs: total_kernel(nta, ngx, scale, *refs),
-        out_shape=array(TMAX, LANES),
+        out_shape=array(LEVELS, TMAX),
         in_specs=[vmem],
         out_specs=vmem,
-        scratch_shapes=[pltpu.VMEM((devices, TMAX, LANES), jnp.float32), sems((devices,)), sems((devices,))],
+        scratch_shapes=[
+            pltpu.VMEM((8, LANES), jnp.float32),
+            pltpu.VMEM((ngx, 8, LANES), jnp.float32),
+            pltpu.VMEM((nta, 8, LANES), jnp.float32),
+            sems((ngx,)),
+            sems((ngx,)),
+            sems((nta,)),
+            sems((nta,)),
+        ],
         compiler_params=remote(2),
         name="total",
     )(part)
-    return flowed.reshape(links.shape), total[:, :LEVELS].T
+    return flowed.reshape(links.shape), total
 
 
 def solution(mesh):

time: 90.5 us -> 77.9 us (0.86)
  local copies, waits for them, and re-layouts: 8.85 us -> 1.86 us
  Pallas kernels: 80.4 us -> 75.2 us
    unnamed x21 -> x5, local copies, waits for them, and re-layouts: 8.18 us -> 1.86 us
    pallas_call x1, Pallas kernels: 20.5 us -> 18.8 us  [body(): pl.pallas_call(lambda *refs: exchange_kernel(nta, ngx, *refs), out_shape=...]
    pallas_call x1, Pallas kernels: 11.4 us -> 9.75 us  [body(): pl.pallas_call(lambda *refs: flow_kernel(slices, split, *refs), out_shape...]
    pallas_call x1, Pallas kernels: 10.5 us -> 9.17 us  [body(): pl.pallas_call(lambda *refs: total_kernel(nta, ngx, scale, *refs), out_sh...]
where the time goes in v2:
time: 77.9 us; the launch traced here: 77.7 us
  Pallas kernels  75.2 us (97%)
  local copies, waits for them, and re-layouts  1.86 us (2%)
    pallas_call x1, Pallas kernels, body(): pl.pallas_call(lambda *refs: halo_kernel(nta, ngx, slices, *refs), out_sh...  21.8 us
    pallas_call x1, Pallas kernels, body(): pl.pallas_call(lambda *refs: exchange_kernel(nta, ngx, *refs), out_shape=...  18.8 us
    pallas_call x1, Pallas kernels, body(): pl.pallas_call(lambda *refs: loop_kernel(nta, 2 * split, *refs), out_shap...  15.7 us
    pallas_call x1, Pallas kernels, body(): pl.pallas_call(lambda *refs: flow_kernel(slices, split, *refs), out_shape...  9.75 us
    pallas_call x1, Pallas kernels, body(): pl.pallas_call(lambda *refs: total_kernel(nta, ngx, scale, *refs), out_sh...  9.17 us
    unnamed x5, local copies, waits for them, and re-layouts  1.86 us

profile of v2, /device:TPU:0, one launch (start us, length us, event | category | flops | bytes accessed | tf_op | source)
XLA Modules:
  0.0 77.7 jit_solution(16337988932506568478)
XLA Ops:
  0.6 0.0 copy-start
  0.6 1.3 %copy-done = f32[4,2,3,3,16,2,128]{6,5,4,3,2,1,0:T(2,128)S(1)} copy-done((f32[4,2,3,3,16,2,128]{6,5,4,3,2,1,0:T(2,128)S(1)}, f32[4,2,3,3,16,2,128]{6,5,4,3,2,1,0:T(2,128)}, u32[]{:S(2)}) %copy-start) | copy-done | bytes 1179672
  1.9 0.0 copy-start.1
  1.9 21.8 %halos.1 = (f32[8,6,16,1,128]{4,3,2,1,0:T(1,128)S(1)}, f32[6,6,16,1,128]{4,3,2,1,0:T(1,128)S(1)}, f32[8,9,2,1,128]{4,3,2,1,0:T(1,128)S(1)}, f32[6,9,2,1,128]{4,3...) custom-call(f32[8,9,16,2,1,128]{5,4,3,2,1,0:T(1,128)S(1)} %bitcast.11), custom_call_target="tpu_custom_call" | custom-call | tf_op jit(solution)/shard_map/halos/pallas_call | solution.py:501
  23.7 0.0 copy-done.1
  23.7 9.8 %flow.1 = (f32[72,32,128]{2,1,0:T(8,128)}, f32[1152,128]{1,0:T(8,128)S(1)}) custom-call(f32[72,32,128]{2,1,0:T(8,128)S(1)} %bitcast.12, f32[48,16,128]{2,1,0:T(8,128)S(1)} %bitcast.15, f32[36,16,128]{2,1,0:T(8,128)S(1)} %bitcast.16, f32[72,2,128]{2,1,0:T(2,128)S(1)} %bitcast.17, f32[54,2,128]{2,1,0:T(2,128)S(1)} %bitcast.18, f32[18,1,128]{2,1,0:T(1,128)S(1)} %bitcast.19, ...), custom_call_target="tpu_custom_call" | custom-call | tf_op jit(solution)/shard_map/flow/pallas_call | solution.py:529
  33.4 18.8 %exchange.1 = f32[32,36,1,128]{3,2,1,0:T(1,128)S(1)} custom-call(f32[32,36,1,128]{3,2,1,0:T(1,128)S(1)} %bitcast.14), custom_call_target="tpu_custom_call" | custom-call | tf_op jit(solution)/shard_map/exchange/pallas_call | solution.py:544
  52.3 15.7 %loops.1.refs_0_ = f32[8,128]{1,0:T(8,128)S(1)} custom-call(f32[1152,128]{1,0:T(8,128)S(1)} %bitcast.13), custom_call_target="tpu_custom_call" | custom-call | tf_op jit(solution)/shard_map/loops/pallas_call | solution.py:557
  67.9 9.2 %total.1 = f32[5,8]{1,0:T(8,128)S(1)} custom-call(f32[8,128]{1,0:T(8,128)S(1)} %loops.1.refs_0_), custom_call_target="tpu_custom_call" | custom-call | tf_op jit(solution)/shard_map/total/pallas_call | solution.py:572
  77.1 0.6 copy.4
Async XLA Ops:
  0.6 1.3 %copy-start = (f32[4,2,3,3,16,2,128]{6,5,4,3,2,1,0:T(2,128)S(1)}, f32[4,2,3,3,16,2,128]{6,5,4,3,2,1,0:T(2,128)}, u32[]{:S(2)}) copy-start(f32[4,2,3,3,16,2,128]{6,5,4,3,2,1,0:T(2,128)} %param.1) | copy-start | bytes 3538948
  1.9 21.8 %copy-start.1 = (f32[4,2,3,3,16,2,128]{6,5,4,3,2,1,0:T(2,128)S(1)}, f32[4,2,3,3,16,2,128]{6,5,4,3,2,1,0:T(2,128)}, u32[]{:S(2)}) copy-start(f32[4,2,3,3,16,2,128]{6,5,4,3,2,1,0:T(2,128)} %param.1) | copy-start | bytes 3538948

commit v3 on v2

--- a/solution.py
+++ b/solution.py
@@ -253,99 +253,92 @@
         pack(g, 0)
 
 
-def loop_kernel(blocks, per_slice, arrived, out, fields, early, lines, ahead):
+def row_product(row, b):
+    out = []
+    for j in range(3):
+        x = [cmul(row[k], b[k][j]) for k in range(3)]
+        out.append((x[0][0] + x[1][0] + x[2][0], x[0][1] + x[1][1] + x[2][1]))
+    return out
+
+
+def loop_kernel(blocks, per_slice, slices, arrived, out, fields, reach, lines):
     groups = fields.shape[2]
     for b in range(blocks):
         for c in range(36):
             fields[c, b] = arrived[pl.ds(36 * groups * b + c, groups, stride=36), :]
-    lane_all = lax.broadcasted_iota(jnp.int32, (groups, LANES), 1)
-    odd = (lane_all & 1) == 1
+    wide = lax.broadcasted_iota(jnp.int32, (groups, LANES), 1)
+    odd = (wide & 1) == 1
+    slot = (wide // per_slice) % slices
     lane = lax.broadcasted_iota(jnp.int32, (8, LANES), 1)
     row = lax.broadcasted_iota(jnp.int32, (8, LANES), 0)
-    slices = 16
+
+    def matrix(get):
+        return [[(get(3 * i + j), get(9 + 3 * i + j)) for j in range(3)] for i in range(3)]
 
     def forward_x(v, distance):
         if distance == 1:
             return jnp.where(odd, roll(roll(v, -1, 0), 1), roll(v, -1))
         return roll(v, -(distance // 2), 0)
 
-    def forward_t(ref, lead, c, b, g, s):
-        own = ref[lead, c, b, pl.ds(g, 8), :]
-        if s == 0:
-            return own
-        following = ref[lead, c, lax.rem(b + 1, blocks), pl.ds(g, 8), :]
-        slot = lane // per_slice if per_slice * slices == LANES else (lane // per_slice) % slices
-        return roll(jnp.where(slot >= s, own, following), -per_slice * s)
+    def forward_t(get, b, s):
+        return roll(jnp.where(slot >= s, get(b), get(lax.rem(b + 1, blocks))), -per_slice * s)
+
+    def temporal(b, _):
+        held = matrix(lambda c: fields[c, b])
+        for s in range(TMAX):
+            if s:
+                held = product(held, matrix(lambda c: forward_t(lambda at: fields[c, at], b, s)))
+            for i in range(3):
+                for j in range(3):
+                    for ri in range(2):
+                        reach[s, 9 * ri + 3 * i + j, b] = held[i][j][ri]
+        return 0
+
+    lax.fori_loop(0, blocks, temporal, 0)
 
     def first(b, _):
         for c in range(18):
             lines[0, c, b] = fields[18 + c, b]
-            ahead[0, c, b] = forward_x(fields[c, b], 1)
         return 0
 
     lax.fori_loop(0, blocks, first, 0)
-    for k in range(1, LEVELS):
-        distance = 2 ** (k - 1)
-
-        def grow(b, _):
-            for c in range(18):
-                ahead[k, c, b] = forward_x(ahead[k - 1, c, b], distance)
-            own = [[(lines[k - 1, 3 * i + j, b], lines[k - 1, 9 + 3 * i + j, b]) for j in range(3)] for i in range(3)]
-            far = [[tuple(forward_x(v, distance) for v in e) for e in row] for row in own]
-            new = product(own, far)
-            for i in range(3):
-                for j in range(3):
-                    for ri in range(2):
-                        lines[k, 9 * ri + 3 * i + j, b] = new[i][j][ri]
-            return 0
-
-        lax.fori_loop(0, blocks, grow, 0)
-
-    def advance(n, _):
-        b = n // (groups // 8)
-        g = pl.multiple_of((n % (groups // 8)) * 8, 8)
-        for s in range(TMAX):
-            for c in range(18):
-                own = fields[c, b, pl.ds(g, 8), :]
-                if s:
-                    following = fields[c, lax.rem(b + 1, blocks), pl.ds(g, 8), :]
-                    own = roll(jnp.where((lane // per_slice) % slices >= s, own, following), -per_slice * s)
-                early[s, c, n] = own
-        return 0
-
-    cells = blocks * (groups // 8)
-    lax.fori_loop(0, cells, advance, 0)
-
-    def level(k, _):
-        def cell(n, totals):
-            b = n // (groups // 8)
-            g = pl.multiple_of((n % (groups // 8)) * 8, 8)
-
-            def matrix(get):
-                return [[(get(3 * i + j), get(9 + 3 * i + j)) for j in range(3)] for i in range(3)]
-
-            carried = matrix(lambda c: forward_t(lines, k, c, b, g, 0))
+    out[...] = jnp.zeros((8, LANES), jnp.float32)
+    for k in range(LEVELS):
+        distance = 2**k
+
+        def cell(b, totals):
+            line = matrix(lambda c: lines[k, c, b])
             new = []
             for extent in range(1, TMAX + 1):
-                s = extent - 1
-                carried = product(matrix(lambda c: early[s, c, n]), carried, da=True)
-                carried = product(carried, matrix(lambda c: forward_t(ahead, k, c, b, g, s)))
-                end = matrix(lambda c: forward_t(lines, k, c, b, g, extent))
-                total = totals[s]
+                near = matrix(lambda c: reach[extent - 1, c, b])
+                far = [[tuple(forward_x(v, distance) for v in e) for e in r] for r in near]
+                end = matrix(lambda c: forward_t(lambda at: lines[k, c, at], b, extent))
+                total = totals[extent - 1]
                 for i in range(3):
-                    for j in range(3):
-                        total = total + (carried[i][j][0] * end[i][j][0] + carried[i][j][1] * end[i][j][1])
+                    upper = row_product(line[i], far)
+                    lower = row_product(near[i], end)
+                    for u, v in zip(upper, lower):
+                        total = total + (u[0] * v[0] + u[1] * v[1])
                 new.append(total)
             return tuple(new)
 
-        totals = lax.fori_loop(0, cells, cell, (jnp.zeros((8, LANES), jnp.float32),) * TMAX)
+        totals = lax.fori_loop(0, blocks, cell, (jnp.zeros((groups, LANES), jnp.float32),) * TMAX)
         block = jnp.concatenate([jnp.sum(t, axis=0, keepdims=True) for t in totals], axis=0)
         spread = jnp.where(lane == row, jnp.sum(block, axis=1, keepdims=True), 0.0)
         out[...] = jnp.where(row == k, jnp.sum(spread, axis=0, keepdims=True), out[...])
-        return 0
-
-    out[...] = jnp.zeros((TMAX, LANES), jnp.float32)
-    lax.fori_loop(0, LEVELS, level, 0)
+        if k + 1 < LEVELS:
+
+            def grow(b, _):
+                own = matrix(lambda c: lines[k, c, b])
+                far = [[tuple(forward_x(v, distance) for v in e) for e in r] for r in own]
+                new = product(own, far)
+                for i in range(3):
+                    for j in range(3):
+                        for ri in range(2):
+                            lines[k + 1, 9 * ri + 3 * i + j, b] = new[i][j][ri]
+                return 0
+
+            lax.fori_loop(0, blocks, grow, 0)
 
 
 MESH = pl.DeviceIdType.MESH
@@ -555,14 +548,13 @@
     if repeats > 1:
         fields = jnp.tile(fields, (1, repeats))
     part = pl.pallas_call(
-        lambda *refs: loop_kernel(nta, 2 * split, *refs),
+        lambda *refs: loop_kernel(nta, 2 * split, slices, *refs),
         out_shape=array(TMAX, LANES),
         in_specs=[vmem],
         out_specs=vmem,
         scratch_shapes=[
             pltpu.VMEM((36, nta, ngx, LANES), jnp.float32),
-            pltpu.VMEM((TMAX, 18, nta * (ngx // 8), 8, LANES), jnp.float32),
-            pltpu.VMEM((LEVELS, 18, nta, ngx, LANES), jnp.float32),
+            pltpu.VMEM((TMAX, 18, nta, ngx, LANES), jnp.float32),
             pltpu.VMEM((LEVELS, 18, nta, ngx, LANES), jnp.float32),
         ],
         compiler_params=pltpu.CompilerParams(vmem_limit_bytes=24 * 2**20),

time: 77.9 us -> 76 us (0.976)
  Pallas kernels: 75.2 us -> 73.3 us
    pallas_call x1, Pallas kernels: 15.7 us -> 13.8 us  [body(): pl.pallas_call(lambda *refs: loop_kernel(nta, 2 * split, slices, *refs),...]
where the time goes in v3:
time: 76 us; the launch traced here: 75.9 us
  Pallas kernels  73.3 us (96%)
  local copies, waits for them, and re-layouts  1.86 us (2%)
    pallas_call x1, Pallas kernels, body(): pl.pallas_call(lambda *refs: halo_kernel(nta, ngx, slices, *refs), out_sh...  21.8 us
    pallas_call x1, Pallas kernels, body(): pl.pallas_call(lambda *refs: exchange_kernel(nta, ngx, *refs), out_shape=...  18.8 us
    pallas_call x1, Pallas kernels, body(): pl.pallas_call(lambda *refs: loop_kernel(nta, 2 * split, slices, *refs),...  13.8 us
    pallas_call x1, Pallas kernels, body(): pl.pallas_call(lambda *refs: flow_kernel(slices, split, *refs), out_shape...  9.75 us
    pallas_call x1, Pallas kernels, body(): pl.pallas_call(lambda *refs: total_kernel(nta, ngx, scale, *refs), out_sh...  9.17 us
    unnamed x5, local copies, waits for them, and re-layouts  1.86 us

profile of v3, /device:TPU:0, one launch (start us, length us, event | category | flops | bytes accessed | tf_op | source)
XLA Modules:
  0.0 75.9 jit_solution(2974859929897489568)
XLA Ops:
  0.6 0.0 copy-start
  0.6 1.3 %copy-done = f32[4,2,3,3,16,2,128]{6,5,4,3,2,1,0:T(2,128)S(1)} copy-done((f32[4,2,3,3,16,2,128]{6,5,4,3,2,1,0:T(2,128)S(1)}, f32[4,2,3,3,16,2,128]{6,5,4,3,2,1,0:T(2,128)}, u32[]{:S(2)}) %copy-start) | copy-done | bytes 1179672
  1.9 0.0 copy-start.1
  1.9 21.8 %halos.1 = (f32[8,6,16,1,128]{4,3,2,1,0:T(1,128)S(1)}, f32[6,6,16,1,128]{4,3,2,1,0:T(1,128)S(1)}, f32[8,9,2,1,128]{4,3,2,1,0:T(1,128)S(1)}, f32[6,9,2,1,128]{4,3...) custom-call(f32[8,9,16,2,1,128]{5,4,3,2,1,0:T(1,128)S(1)} %bitcast.11), custom_call_target="tpu_custom_call" | custom-call | tf_op jit(solution)/shard_map/halos/pallas_call | solution.py:494
  23.7 0.0 copy-done.1
  23.7 9.8 %flow.1 = (f32[72,32,128]{2,1,0:T(8,128)}, f32[1152,128]{1,0:T(8,128)S(1)}) custom-call(f32[72,32,128]{2,1,0:T(8,128)S(1)} %bitcast.12, f32[48,16,128]{2,1,0:T(8,128)S(1)} %bitcast.15, f32[36,16,128]{2,1,0:T(8,128)S(1)} %bitcast.16, f32[72,2,128]{2,1,0:T(2,128)S(1)} %bitcast.17, f32[54,2,128]{2,1,0:T(2,128)S(1)} %bitcast.18, f32[18,1,128]{2,1,0:T(1,128)S(1)} %bitcast.19, ...), custom_call_target="tpu_custom_call" | custom-call | tf_op jit(solution)/shard_map/flow/pallas_call | solution.py:522
  33.4 18.8 %exchange.1 = f32[32,36,1,128]{3,2,1,0:T(1,128)S(1)} custom-call(f32[32,36,1,128]{3,2,1,0:T(1,128)S(1)} %bitcast.14), custom_call_target="tpu_custom_call" | custom-call | tf_op jit(solution)/shard_map/exchange/pallas_call | solution.py:537
  52.3 13.8 %loops.1.refs_0_ = f32[8,128]{1,0:T(8,128)S(1)} custom-call(f32[1152,128]{1,0:T(8,128)S(1)} %bitcast.13), custom_call_target="tpu_custom_call" | custom-call | tf_op jit(solution)/shard_map/loops/pallas_call | solution.py:550
  66.1 9.2 %total.1 = f32[5,8]{1,0:T(8,128)S(1)} custom-call(f32[8,128]{1,0:T(8,128)S(1)} %loops.1.refs_0_), custom_call_target="tpu_custom_call" | custom-call | tf_op jit(solution)/shard_map/total/pallas_call | solution.py:564
  75.3 0.6 copy.4
Async XLA Ops:
  0.6 1.3 %copy-start = (f32[4,2,3,3,16,2,128]{6,5,4,3,2,1,0:T(2,128)S(1)}, f32[4,2,3,3,16,2,128]{6,5,4,3,2,1,0:T(2,128)}, u32[]{:S(2)}) copy-start(f32[4,2,3,3,16,2,128]{6,5,4,3,2,1,0:T(2,128)} %param.1) | copy-start | bytes 3538948
  1.9 21.8 %copy-start.1 = (f32[4,2,3,3,16,2,128]{6,5,4,3,2,1,0:T(2,128)S(1)}, f32[4,2,3,3,16,2,128]{6,5,4,3,2,1,0:T(2,128)}, u32[]{:S(2)}) copy-start(f32[4,2,3,3,16,2,128]{6,5,4,3,2,1,0:T(2,128)} %param.1) | copy-start | bytes 3538948
